TPU v7x, 32 devices: a whole 2x2x4 slice. The times are simulated.
32 devices in a mesh: prompt: 4 (over y, x), resp: 8 (over z, core).
Axes of the slice: x: 2, y: 2, z: 4, core: 2. Of those that a mesh axis runs over, the one named last changes fastest.
Arguments:
- question_key_matrix: bfloat16 [8, 1024, 256], P('resp', 'prompt'), may hold values from -0.31835938 to 0.31835938
- prompt_values: bfloat16 [8, 1024, 256], P('resp', 'prompt'), may hold values from -6 to 6
- prompt_gates: float32 [8, 2, 1024], P('resp', None, 'prompt'), may hold values from -2.3 to 0, as said below
- resp_queries: bfloat16 [128, 512, 256], P(('prompt', 'resp')), may hold values from -0.31835938 to 0.31835938
- resp_keys: bfloat16 [128, 512, 256], P(('prompt', 'resp')), may hold values from -0.31835938 to 0.31835938
- response_value_rows: bfloat16 [128, 512, 256], P(('prompt', 'resp')), may hold values from -6 to 6
- resp_gates: float32 [128, 2, 512], P(('prompt', 'resp')), may hold values from -2.3 to 0, as said below
- resp_cotangent: bfloat16 [128, 512, 256], P(('prompt', 'resp')), may hold values from -0.59765625 to 0.59765625
- group_ids: int32 [128], P(('prompt', 'resp')), may hold values from 0 to 7, as said below
- resp_lengths: int32 [32, 4], P(('prompt', 'resp')), may hold values from 1 to 512, 1536 in all within a row
- loss_mask: int32 [128, 512], P(('prompt', 'resp')), may hold values 0 or 1
- advantages: int32 [128], P(('prompt', 'resp')), may hold values from -2048 to 2048
Outputs:
- resp_out: bfloat16 [128, 512, 256], P(('prompt', 'resp'))
- resp_dq: bfloat16 [128, 512, 256], P(('prompt', 'resp'))
- answer_key_derivative: bfloat16 [128, 512, 256], P(('prompt', 'resp'))
- resp_dv: bfloat16 [128, 512, 256], P(('prompt', 'resp'))
- prompt_dk: bfloat16 [8, 1024, 256], P('resp', 'prompt')
- prompt_dv: bfloat16 [8, 1024, 256], P('resp', 'prompt')
Inputs may be any that keep to these rules, and one draw needn't show every extreme that they name: `group_ids`: never falling along the responses; every prompt has at least one response. `resp_lengths`: the lengths of one device's 4 responses sum to 1536. `prompt_gates`: negative log decays. `resp_gates`: negative log decays.
All inputs are finite; a program needn't handle non-finite values. No bound on the sum of `loss_mask` on one device may be relied on, other than what follows from the above.
Results may differ from a plain program's by a relative error of at most 0.012.
Values may be sent and summed in bfloat16 or wider, within the bound.
No kernel may reach another device: no remote copies, remote signals or barrier semaphores. Data moves between devices by JAX's collectives and lax.ppermute only.
A program may use at most 64 MiB of HBM per device.

v0:
```python
import jax
import jax.numpy as jnp
from jax import lax
from jax.experimental import pallas as pl
from jax.experimental.pallas import tpu as pltpu
from jax.sharding import PartitionSpec as P

H = 2
DH = 128
HALF = 256
F32 = jnp.float32
BF16 = jnp.bfloat16
NEVER = -1e30
VMEM = pl.BlockSpec(memory_space=pltpu.VMEM)
SMEM = pl.BlockSpec(memory_space=pltpu.SMEM)


def params(mebibytes=62):
    return pltpu.CompilerParams(vmem_limit_bytes=mebibytes * 1024 * 1024)


def mm(a, b):
    return lax.dot_general(a, b, (((1,), (0,)), ((), ())), preferred_element_type=F32)


def mm_nt(a, b):
    return lax.dot_general(a, b, (((1,), (1,)), ((), ())), preferred_element_type=F32)


def mm_tn(a, b):
    return lax.dot_general(a, b, (((0,), (0,)), ((), ())), preferred_element_type=F32)


def lane_cumsum(x):
    width = x.shape[1]
    lane = lax.broadcasted_iota(jnp.int32, x.shape, 1)
    step = 1
    while step < width:
        x = x + jnp.where(lane >= step, pltpu.roll(x, step, 1), 0.0)
        step *= 2
    return x


def to_columns(rows):
    padded = jnp.concatenate([rows, jnp.zeros((128 - rows.shape[0], rows.shape[1]), F32)], axis=0)
    return padded.T


def first_kernel(
    n, ids_ref, lens_ref, adv_ref, keys_hbm, values_hbm, pgates_hbm, gates_hbm, mask_hbm, q_hbm, c_hbm,
    msg_ref, suffix_ref, cols_ref, rows_ref,
    keys, values, pgates, gates, mask, q, c, sems,
):
    pairs = [(pgates_hbm, pgates), (keys_hbm, keys), (values_hbm, values), (gates_hbm, gates), (mask_hbm, mask)]
    count = gates.shape[0]
    slots = gates.shape[2]
    for i in range(count):
        pairs += [(q_hbm.at[i], q.at[i]), (c_hbm.at[i], c.at[i])]
    copies = [pltpu.make_async_copy(a, b, sems.at[i]) for i, (a, b) in enumerate(pairs)]
    for copy in copies:
        copy.start()
    for copy in copies[:3]:
        copy.wait()
    part = DH // n
    piece = pgates[0]
    cum = lane_cumsum(jnp.concatenate([piece, jnp.zeros((8 - H, piece.shape[1]), F32)], axis=0))
    total = cum[:, -1:]
    suffix = to_columns(total - cum)
    suffix_ref[...] = suffix
    for h in range(H):
        lanes = slice(h * DH, (h + 1) * DH)
        scaled = jnp.exp(suffix[:, h : h + 1]) * values[0, :, lanes].astype(F32)
        high = scaled.astype(BF16)
        low = (scaled - high.astype(F32)).astype(BF16)
        both = mm_tn(keys[0, :, lanes], jnp.concatenate([high, low], axis=1))
        state = (both[:, :DH] + both[:, DH:]).astype(BF16)
        for k in range(n):
            msg_ref[k, h * part : (h + 1) * part, :] = state[k * part : (k + 1) * part]
    high = total.astype(BF16).astype(F32)
    middle = (total - high).astype(BF16).astype(F32)
    low = total - high - middle
    notes = [jnp.broadcast_to(x[h : h + 1], (1, DH)) for x in (high, middle, low) for h in range(H)]
    notes += [jnp.full((1, DH), ids_ref[i].astype(F32)) for i in range(count)]
    notes.append(jnp.zeros((16 - len(notes), DH), F32))
    notes = jnp.concatenate(notes, axis=0).astype(BF16)
    for k in range(n):
        msg_ref[k, H * part : H * part + 16, :] = notes

    for copy in copies[3:5]:
        copy.wait()
    cum = lane_cumsum(jnp.concatenate([gates[i] for i in range(count)], axis=0))
    carried = jnp.exp(cum)
    place = lax.broadcasted_iota(jnp.int32, (1, slots), 1)
    rows = []
    for i in range(count):
        weight = adv_ref[i].astype(F32) / 1024.0
        opened = jnp.where(place < lens_ref[0, i], 1.0, 0.0)
        live = mask[i : i + 1, :].astype(F32) * opened * weight
        rows += [cum[H * i : H * i + H], carried[H * i : H * i + H], live, opened, jnp.zeros((2, slots), F32)]
    rows = jnp.concatenate(rows, axis=0)
    rows_ref[...] = rows.reshape(count, 8, slots)
    cols = to_columns(rows)
    cols_ref[...] = cols
    for i in range(count):
        copies[5 + 2 * i].wait()
        copies[6 + 2 * i].wait()
        for h in range(H):
            lanes = slice(h * DH, (h + 1) * DH)
            grad_out = (c[i, :, lanes].astype(F32) * cols[:, 8 * i + 4 : 8 * i + 5]).astype(BF16)
            scaled = (cols[:, 8 * i + 2 + h : 8 * i + 3 + h] * grad_out.astype(F32)).astype(BF16)
            grad = mm_tn(q[i, :, lanes], scaled).astype(BF16)
            for k in range(n):
                at = H * part + 16 + (i * H + h) * part
                msg_ref[k, at : at + part, :] = grad[k * part : (k + 1) * part]


def pick(ids, p):
    return jnp.where(ids == p, 1.0, 0.0)


def second_kernel(n, count, me_ref, got_ref, msg_ref, later_ref, sums):
    part = DH // n
    block = H * part
    notes = [got_ref[k, block : block + 16, :].astype(F32) for k in range(n)]
    logs = [x[0:H] + x[H : 2 * H] + x[2 * H : 3 * H] for x in notes]
    final = [None] * H
    later = jnp.zeros_like(logs[0])
    mine = jnp.zeros_like(logs[0])
    for k in range(n - 1, -1, -1):
        mine = jnp.where(me_ref[0] == k, later, mine)
        decay = jnp.exp(later)
        for h in range(H):
            term = decay[h : h + 1] * got_ref[k, h * part : (h + 1) * part, :].astype(F32)
            final[h] = term if final[h] is None else final[h] + term
        later = later + logs[k]
    later_ref[...] = jnp.concatenate([mine, jnp.zeros((8 - H, DH), F32)], axis=0)
    final = jnp.concatenate(final, axis=0).astype(BF16)
    sums[...] = jnp.zeros_like(sums)
    responses = (got_ref.shape[1] - block - 16) // block
    for k in range(n):
        for i in range(responses):
            at = block + 16 + i * block
            p = jnp.max(notes[k][3 * H + i : 3 * H + i + 1]).astype(jnp.int32)
            sums[p] += got_ref[k, at : at + block, :].astype(F32)
    for p in range(count):
        msg_ref[p, 0:block, :] = final
        msg_ref[p, block : 2 * block, :] = sums[p].astype(BF16)


def third_kernel(n, count, first_ref, got_ref, msg_ref):
    part = DH // n
    block = H * part
    responses = (first_ref.shape[1] - block - 16) // block
    total = got_ref[0, block:, :].astype(F32)
    for p in range(1, count):
        total = total + got_ref[p, block:, :].astype(F32)
    total = total.astype(BF16)
    for k in range(n):
        notes = first_ref[k, block : block + 16, :].astype(F32)
        for i in range(responses):
            p = jnp.max(notes[3 * H + i : 3 * H + i + 1]).astype(jnp.int32)
            msg_ref[k, i * block : (i + 1) * block, :] = got_ref[p, 0:block, :]
        msg_ref[k, responses * block :, :] = total


def sweep_kernel(cols_ref, rows_ref, q_ref, k_ref, v_ref, c_ref, out_ref, dq_ref, dk_ref, dv_ref):
    r = pl.program_id(0)
    mine = pltpu.roll(cols_ref[...], lax.rem(128 - 8 * r, 128), 1)
    rows = rows_ref[0]
    live = mine[:, 4:5]
    causal = lax.broadcasted_iota(jnp.int32, (HALF, HALF), 0) >= lax.broadcasted_iota(
        jnp.int32, (HALF, HALF), 1
    )
    blocks = q_ref.shape[1] // HALF
    for h in range(H):
        lanes = slice(h * DH, (h + 1) * DH)
        cum = mine[:, h : h + 1]
        dk = [None] * blocks
        dv = [None] * blocks
        for t in range(blocks):
            at = slice(t * HALF, (t + 1) * HALF)
            query = q_ref[0, at, lanes]
            grad_out = (c_ref[0, at, lanes].astype(F32) * live[at]).astype(BF16)
            out = None
            dq = None
            for s in range(t + 1):
                of = slice(s * HALF, (s + 1) * HALF)
                key = k_ref[0, of, lanes]
                value = v_ref[0, of, lanes]
                diff = cum[at] - rows[h : h + 1, of]
                if s == t:
                    diff = jnp.where(causal, diff, NEVER)
                decay = jnp.exp(diff)
                mixing = (mm_nt(query, key) * decay).astype(BF16)
                scores = (mm_nt(grad_out, value) * decay).astype(BF16)
                o_new = mm(mixing, value)
                q_new = mm(scores, key)
                k_new = mm_tn(scores, query)
                v_new = mm_tn(mixing, grad_out)
                out = o_new if out is None else out + o_new
                dq = q_new if dq is None else dq + q_new
                dk[s] = k_new if dk[s] is None else dk[s] + k_new
                dv[s] = v_new if dv[s] is None else dv[s] + v_new
            out_ref[0, at, lanes] = out
            dq_ref[0, at, lanes] = dq
        for s in range(blocks):
            of = slice(s * HALF, (s + 1) * HALF)
            dk_ref[0, of, lanes] = dk[s].astype(BF16)
            dv_ref[0, of, lanes] = dv[s].astype(BF16)


def last_kernel(
    n, steps, cols_ref, q_ref, c_ref, po_ref, pdq_ref, got_ref, keys_ref, values_ref, suffix_ref, later_ref,
    out_ref, dq_ref, dk_ref, dv_ref, start,
):
    r = pl.program_id(0)
    part = DH // n
    for k in range(n):
        for h in range(H):
            at = pl.multiple_of((r * H + h) * part, part)
            start[h, k * part : (k + 1) * part, :] = got_ref[k, pl.ds(at, part), :]
    mine = pltpu.roll(cols_ref[...], lax.rem(128 - 8 * r, 128), 1)
    live = mine[:, 4:5]
    opened = mine[:, 5:6]
    for h in range(H):
        lanes = slice(h * DH, (h + 1) * DH)
        carried = mine[:, 2 + h : 3 + h]
        grad_out = (c_ref[0, :, lanes].astype(F32) * live).astype(BF16)
        out = po_ref[0, :, lanes] + carried * mm(q_ref[0, :, lanes], start[h])
        out_ref[0, :, lanes] = (opened * out).astype(BF16)
        dq = pdq_ref[0, :, lanes] + carried * mm_nt(grad_out, start[h])
        dq_ref[0, :, lanes] = dq.astype(BF16)

    @pl.when(r == 0)
    def _():
        for h in range(H):
            lanes = slice(h * DH, (h + 1) * DH)
            at = (steps * H + h) * part
            grad = jnp.concatenate([got_ref[k, at : at + part, :] for k in range(n)], axis=0)
            factor = jnp.exp(suffix_ref[:, h : h + 1] + later_ref[h : h + 1, 0:1])
            dk_ref[0, :, lanes] = (factor * mm_nt(values_ref[0, :, lanes], grad)).astype(BF16)
            dv_ref[0, :, lanes] = (factor * mm(keys_ref[0, :, lanes], grad)).astype(BF16)


def exchange(x, axis):
    return lax.all_to_all(x, axis, 0, 0, tiled=True)


def shards(
    keys,
    values,
    prompt_gates,
    queries,
    resp_keys,
    resp_values,
    resp_gates,
    cotangent,
    group_ids,
    resp_lengths,
    loss_mask,
    advantages,
):
    n = lax.axis_size("prompt")
    count = lax.axis_size("resp")
    row = lax.axis_index("prompt").astype(jnp.int32)[None]
    responses, slots, width = queries.shape
    block_rows = H * DH // n
    tokens = keys.shape[1]
    shape = jax.ShapeDtypeStruct
    HBM = pl.BlockSpec(memory_space=pltpu.HBM)

    msg, suffix, cols, rows = pl.pallas_call(
        lambda *refs: first_kernel(n, *refs),
        out_shape=[
            shape((n, block_rows * (1 + responses) + 16, DH), BF16),
            shape((tokens, 128), F32),
            shape((slots, 128), F32),
            shape((responses, 8, slots), F32),
        ],
        in_specs=[SMEM] * 3 + [HBM] * 7,
        out_specs=[VMEM] * 4,
        scratch_shapes=[
            pltpu.VMEM(keys.shape, BF16),
            pltpu.VMEM(values.shape, BF16),
            pltpu.VMEM(prompt_gates.shape, F32),
            pltpu.VMEM(resp_gates.shape, F32),
            pltpu.VMEM(loss_mask.shape, jnp.int32),
            pltpu.VMEM(queries.shape, BF16),
            pltpu.VMEM(queries.shape, BF16),
            pltpu.SemaphoreType.DMA((5 + 2 * responses,)),
        ],
        compiler_params=params(),
        name="first",
    )(
        group_ids, resp_lengths, advantages, keys, values, prompt_gates, resp_gates, loss_mask, queries, cotangent
    )
    got1 = exchange(msg, "prompt")
    msg, later = pl.pallas_call(
        lambda *refs: second_kernel(n, count, *refs),
        out_shape=[shape((count, 2 * block_rows, DH), BF16), shape((8, DH), F32)],
        in_specs=[SMEM, VMEM],
        out_specs=[VMEM, VMEM],
        scratch_shapes=[pltpu.VMEM((count, block_rows, DH), F32)],
        compiler_params=params(16),
        name="second",
    )(row, got1)
    got2 = exchange(msg, "resp")
    msg = pl.pallas_call(
        lambda *refs: third_kernel(n, count, *refs),
        out_shape=shape((n, (responses + 1) * block_rows, DH), BF16),
        in_specs=[VMEM, VMEM],
        out_specs=VMEM,
        compiler_params=params(16),
        name="third",
    )(got1, got2)
    got3 = exchange(msg, "prompt")

    block = pl.BlockSpec((1, slots, width), lambda r: (r, 0, 0))
    lane_block = pl.BlockSpec((slots, 128), lambda r: (0, 0))
    row_block = pl.BlockSpec((1, 8, slots), lambda r: (r, 0, 0))
    like = shape(queries.shape, F32)
    like_out = shape(queries.shape, BF16)
    partial_out, partial_dq, resp_dk, resp_dv = pl.pallas_call(
        sweep_kernel,
        grid=(responses,),
        out_shape=[like, like, like_out, like_out],
        in_specs=[lane_block, row_block, block, block, block, block],
        out_specs=[block] * 4,
        compiler_params=params(),
        name="sweep",
    )(cols, rows, queries, resp_keys, resp_values, cotangent)

    resp_out, resp_dq, prompt_dk, prompt_dv = pl.pallas_call(
        lambda *refs: last_kernel(n, responses, *refs),
        grid=(responses,),
        out_shape=[like_out, like_out, shape(keys.shape, BF16), shape(keys.shape, BF16)],
        in_specs=[lane_block, block, block, block, block] + [VMEM] * 5,
        out_specs=[block, block, VMEM, VMEM],
        scratch_shapes=[pltpu.VMEM((H, DH, DH), BF16)],
        compiler_params=params(),
        name="last",
    )(cols, queries, cotangent, partial_out, partial_dq, got3, keys, values, suffix, later)
    return (resp_out, resp_dq, resp_dk, resp_dv, prompt_dk, prompt_dv)


def solution(mesh):
    spread = P(("prompt", "resp"))
    three = P(("prompt", "resp"), None, None)
    two = P(("prompt", "resp"), None)
    prompt = P("resp", "prompt", None)
    return jax.shard_map(
        shards,
        mesh=mesh,
        in_specs=(
            prompt,
            prompt,
            P("resp", None, "prompt"),
            three,
            three,
            three,
            three,
            three,
            spread,
            two,
            two,
            spread,
        ),
        out_specs=(three, three, three, three, prompt, prompt),
        check_vma=False,
    )
```

profile of v0, /device:TPU:0, one launch (start us, length us, event | category | flops | bytes accessed | tf_op | source)
XLA Modules:
  0.0 56.1 jit_solution(1236926648691164877)
XLA Ops:
  0.6 6.1 %first.1 = (bf16[4,336,128]{2,1,0:T(8,128)(2,1)}, f32[256,128]{1,0:T(8,128)}, f32[512,128]{1,0:T(8,128)}, f32[4,8,512]{2,1,0:T(8,128)}) custom-call(s32[4]{0:T(128)} %refs_0_.1, s32[1,4]{1,0:T(1,128)} %refs_1_.2, s32[4]{0:T(128)} %refs_2_.2, bf16[1,256,256]{2,1,0:T(8,128)(2,1)} %refs_6_.3, bf16[1,256,256]{2,1,0:T(8,128)(2,1)} %refs_7_.3, ...), custom_call_target="tpu_custom_call" | custom-call | tf_op jit(solution)/shard_map/first/pallas_call | solution.py:272
  6.8 5.2 %all-to-all-start = ((bf16[4,336,128]{2,1,0:T(8,128)(2,1)}), bf16[4,336,128]{2,1,0:T(8,128)(2,1)S(1)}, u32[]{:S(2)}, u32[]{:S(2)}) async-start(bf16[4,336,128]{2,1,0:T(8,128)(2,1)} %get-tuple-element.24), calls=%async_computation | async-start | bytes 688128 | tf_op jit(solution)/shard_map/all_to_all | solution.py:246
  11.9 6.0 %all-to-all-done.refs_1_.refs_0_ = bf16[4,336,128]{2,1,0:T(8,128)(2,1)S(1)} async-done(((bf16[4,336,128]{2,1,0:T(8,128)(2,1)}), bf16[4,336,128]{2,1,0:T(8,128)(2,1)S(1)}, u32[]{:S(2)}, u32[]{:S(2)}) %all-to-all-start) | async-done | bytes 344096 | tf_op jit(solution)/shard_map/all_to_all | solution.py:246
  18.0 0.2 second.1
  18.2 0.0 copy-start
  18.2 0.6 %copy-done = f32[8,128]{1,0:T(8,128)} copy-done((f32[8,128]{1,0:T(8,128)}, f32[8,128]{1,0:T(8,128)S(1)}, u32[]{:S(2)}) %copy-start) | copy-done | bytes 4120
  18.8 14.4 %all_to_all.15.refs_1_ = bf16[8,128,128]{2,1,0:T(8,128)(2,1)S(1)} all-to-all(bf16[8,128,128]{2,1,0:T(8,128)(2,1)S(1)} %get-tuple-element.25), channel_id=1, replica_groups=mesh['prompt'=4,'resp'=8] {'resp'}, dimensions={0} | all-to-all | bytes 524288 | tf_op jit(solution)/shard_map/all_to_all | solution.py:246
  33.2 0.9 %third.1 = bf16[4,320,128]{2,1,0:T(8,128)(2,1)} custom-call(bf16[4,336,128]{2,1,0:T(8,128)(2,1)S(1)} %all-to-all-done.refs_1_.refs_0_, bf16[8,128,128]{2,1,0:T(8,128)(2,1)S(1)} %all_to_all.15.refs_1_), custom_call_target="tpu_custom_call" | custom-call | tf_op jit(solution)/shard_map/third/pallas_call | solution.py:308
  34.1 3.5 %all-to-all-start.2 = ((bf16[4,320,128]{2,1,0:T(8,128)(2,1)}), bf16[4,320,128]{2,1,0:T(8,128)(2,1)S(1)}, u32[]{:S(2)}, u32[]{:S(2)}) async-start(bf16[4,320,128]{2,1,0:T(8,128)(2,1)} %third.1), calls=%async_computation.2 | async-start | bytes 655360 | tf_op jit(solution)/shard_map/all_to_all | solution.py:246
  37.5 11.8 %sweep.1 = (f32[4,512,256]{2,1,0:T(8,128)}, f32[4,512,256]{2,1,0:T(8,128)}, bf16[4,512,256]{2,1,0:T(8,128)(2,1)}, bf16[4,512,256]{2,1,0:T(8,128)(2,1)}) custom-call(f32[512,128]{1,0:T(8,128)} %get-tuple-element.20.cols_ref.refs_0_, f32[4,8,512]{2,1,0:T(8,128)} %get-tuple-element.21.rows_ref, bf16[4,512,256]{2,1,0:T(8,128)(2,1)} %refs_1_.3, ...), custom_call_target="tpu_custom_call" | custom-call | tf_op jit(solution)/shard_map/sweep/pallas_call | solution.py:323
  49.3 0.0 all-to-all-done.2.refs_5_
  49.4 0.0 copy-start.1
  49.4 0.7 %copy-done.1 = bf16[4,320,128]{2,1,0:T(8,128)(2,1)} copy-done((bf16[4,320,128]{2,1,0:T(8,128)(2,1)}, bf16[4,320,128]{2,1,0:T(8,128)(2,1)S(1)}, u32[]{:S(2)}) %copy-start.1) | copy-done | bytes 327704
  50.1 6.0 %last.1 = (bf16[4,512,256]{2,1,0:T(8,128)(2,1)}, bf16[4,512,256]{2,1,0:T(8,128)(2,1)}, bf16[1,256,256]{2,1,0:T(8,128)(2,1)}, bf16[1,256,256]{2,1,0:T(8,128)(2,1)}) custom-call(f32[512,128]{1,0:T(8,128)} %get-tuple-element.20.cols_ref.refs_0_, bf16[4,512,256]{2,1,0:T(8,128)(2,1)} %refs_1_.3, bf16[4,512,256]{2,1,0:T(8,128)(2,1)} %refs_2_.3, ...), custom_call_target="tpu_custom_call" | custom-call | tf_op jit(solution)/shard_map/last/pallas_call | solution.py:333
Async XLA Ops:
  6.8 11.2 %all-to-all-start = ((bf16[4,336,128]{2,1,0:T(8,128)(2,1)}), bf16[4,336,128]{2,1,0:T(8,128)(2,1)S(1)}, u32[]{:S(2)}, u32[]{:S(2)}) async-start(bf16[4,336,128]{2,1,0:T(8,128)(2,1)} %get-tuple-element.24), calls=%async_computation | async-start | bytes 688128 | tf_op jit(solution)/shard_map/all_to_all | solution.py:246
  18.2 0.6 %copy-start = (f32[8,128]{1,0:T(8,128)}, f32[8,128]{1,0:T(8,128)S(1)}, u32[]{:S(2)}) copy-start(f32[8,128]{1,0:T(8,128)S(1)} %get-tuple-element.27.refs_9_) | copy-start | bytes 12292
  34.1 15.3 %all-to-all-start.2 = ((bf16[4,320,128]{2,1,0:T(8,128)(2,1)}), bf16[4,320,128]{2,1,0:T(8,128)(2,1)S(1)}, u32[]{:S(2)}, u32[]{:S(2)}) async-start(bf16[4,320,128]{2,1,0:T(8,128)(2,1)} %third.1), calls=%async_computation.2 | async-start | bytes 655360 | tf_op jit(solution)/shard_map/all_to_all | solution.py:246
  49.4 0.7 %copy-start.1 = (bf16[4,320,128]{2,1,0:T(8,128)(2,1)}, bf16[4,320,128]{2,1,0:T(8,128)(2,1)S(1)}, u32[]{:S(2)}) copy-start(bf16[4,320,128]{2,1,0:T(8,128)(2,1)S(1)} %all-to-all-done.2.refs_5_) | copy-start | bytes 983044
where the time goes:
time: 56.5 us; the launch traced here: 56.1 us
  Pallas kernels  25.1 us (44%)
  blocking collectives  14.4 us (25%)
  starting transfers between devices  8.63 us (15%)
  waiting for transfers between devices  6.05 us (11%)
  local copies, waits for them, and re-layouts  1.29 us (2%)
  between operations  0.68 us (1%)
    all_to_all x1, blocking collectives, exchange(): return lax.all_to_all(x, axis, 0, 0, tiled=True)  14.4 us
    pallas_call x1, Pallas kernels, shards(): pl.pallas_call(sweep_kernel, grid=(responses,), out_shape=[like, like, li...  11.8 us
    all_to_all x2, starting transfers between devices, exchange(): return lax.all_to_all(x, axis, 0, 0, tiled=True)  8.63 us
    pallas_call x1, Pallas kernels, shards(): pl.pallas_call(lambda *refs: first_kernel(n, *refs), out_shape=[shape((n,...  6.11 us
    all_to_all x2, waiting for transfers between devices, exchange(): return lax.all_to_all(x, axis, 0, 0, tiled=True)  6.05 us
    pallas_call x1, Pallas kernels, shards(): pl.pallas_call(lambda *refs: last_kernel(n, responses, *refs), grid=(resp...  6.04 us
    unnamed x4, local copies, waits for them, and re-layouts  1.29 us
  transfers between devices with their start and end apart: 2, of which 1 were waited for; matrix products, arithmetic and copies ran while one was open for 0% of the time, Pallas kernels for 21%

commit v1 on v0

--- a/solution.py
+++ b/solution.py
@@ -46,8 +46,19 @@
     return padded.T
 
 
+def row_block(matrices, k, m):
+    part = DH // m
+    return jnp.concatenate([x[k * part : (k + 1) * part] for x in matrices], axis=0).astype(BF16)
+
+
+def from_blocks(blocks, h):
+    part = blocks[0].shape[0] // H
+    rows = [x.astype(F32)[h * part : (h + 1) * part] for x in blocks]
+    return jnp.concatenate(rows, axis=0).astype(BF16)
+
+
 def first_kernel(
-    n, ids_ref, lens_ref, adv_ref, keys_hbm, values_hbm, pgates_hbm, gates_hbm, mask_hbm, q_hbm, c_hbm,
+    m, ids_ref, lens_ref, adv_ref, keys_hbm, values_hbm, pgates_hbm, gates_hbm, mask_hbm, q_hbm, c_hbm,
     msg_ref, suffix_ref, cols_ref, rows_ref,
     keys, values, pgates, gates, mask, q, c, sems,
 ):
@@ -61,21 +72,22 @@
         copy.start()
     for copy in copies[:3]:
         copy.wait()
-    part = DH // n
+    block = H * DH // m
     piece = pgates[0]
     cum = lane_cumsum(jnp.concatenate([piece, jnp.zeros((8 - H, piece.shape[1]), F32)], axis=0))
     total = cum[:, -1:]
     suffix = to_columns(total - cum)
     suffix_ref[...] = suffix
+    states = []
     for h in range(H):
         lanes = slice(h * DH, (h + 1) * DH)
         scaled = jnp.exp(suffix[:, h : h + 1]) * values[0, :, lanes].astype(F32)
         high = scaled.astype(BF16)
         low = (scaled - high.astype(F32)).astype(BF16)
         both = mm_tn(keys[0, :, lanes], jnp.concatenate([high, low], axis=1))
-        state = (both[:, :DH] + both[:, DH:]).astype(BF16)
-        for k in range(n):
-            msg_ref[k, h * part : (h + 1) * part, :] = state[k * part : (k + 1) * part]
+        states.append(both[:, :DH] + both[:, DH:])
+    for k in range(m):
+        msg_ref[k, 0:block, :] = row_block(states, k, m)
     high = total.astype(BF16).astype(F32)
     middle = (total - high).astype(BF16).astype(F32)
     low = total - high - middle
@@ -83,8 +95,8 @@
     notes += [jnp.full((1, DH), ids_ref[i].astype(F32)) for i in range(count)]
     notes.append(jnp.zeros((16 - len(notes), DH), F32))
     notes = jnp.concatenate(notes, axis=0).astype(BF16)
-    for k in range(n):
-        msg_ref[k, H * part : H * part + 16, :] = notes
+    for k in range(m):
+        msg_ref[k, block : block + 16, :] = notes
 
     for copy in copies[3:5]:
         copy.wait()
@@ -104,63 +116,69 @@
     for i in range(count):
         copies[5 + 2 * i].wait()
         copies[6 + 2 * i].wait()
+        grads = []
         for h in range(H):
             lanes = slice(h * DH, (h + 1) * DH)
             grad_out = (c[i, :, lanes].astype(F32) * cols[:, 8 * i + 4 : 8 * i + 5]).astype(BF16)
             scaled = (cols[:, 8 * i + 2 + h : 8 * i + 3 + h] * grad_out.astype(F32)).astype(BF16)
-            grad = mm_tn(q[i, :, lanes], scaled).astype(BF16)
-            for k in range(n):
-                at = H * part + 16 + (i * H + h) * part
-                msg_ref[k, at : at + part, :] = grad[k * part : (k + 1) * part]
-
-
-def pick(ids, p):
-    return jnp.where(ids == p, 1.0, 0.0)
-
-
-def second_kernel(n, count, me_ref, got_ref, msg_ref, later_ref, sums):
-    part = DH // n
-    block = H * part
-    notes = [got_ref[k, block : block + 16, :].astype(F32) for k in range(n)]
+            grads.append(mm_tn(q[i, :, lanes], scaled))
+        at = block * (1 + i) + 16
+        for k in range(m):
+            msg_ref[k, at : at + block, :] = row_block(grads, k, m)
+
+
+def noted_prompt(notes, i):
+    return jnp.max(notes[3 * H + i : 3 * H + i + 1]).astype(jnp.int32)
+
+
+def second_kernel(m, chips, me_ref, got_ref, msg_ref, later_ref, sums):
+    cores = msg_ref.shape[1] * m // (2 * H * DH)
+    block = H * DH // m
+    responses = (got_ref.shape[1] - block - 16) // block
+    notes = [got_ref[k, block : block + 16, :].astype(F32) for k in range(m)]
     logs = [x[0:H] + x[H : 2 * H] + x[2 * H : 3 * H] for x in notes]
-    final = [None] * H
-    later = jnp.zeros_like(logs[0])
     mine = jnp.zeros_like(logs[0])
-    for k in range(n - 1, -1, -1):
-        mine = jnp.where(me_ref[0] == k, later, mine)
-        decay = jnp.exp(later)
-        for h in range(H):
-            term = decay[h : h + 1] * got_ref[k, h * part : (h + 1) * part, :].astype(F32)
-            final[h] = term if final[h] is None else final[h] + term
-        later = later + logs[k]
+    for c in range(cores):
+        final = jnp.zeros((block, DH), F32)
+        later = jnp.zeros_like(logs[0])
+        for k in range(m - cores + c, -1, -cores):
+            mine = jnp.where(me_ref[0] == k, later, mine)
+            decay = jnp.exp(later)
+            decay = [jnp.broadcast_to(decay[h : h + 1], (block // H, DH)) for h in range(H)]
+            final = final + jnp.concatenate(decay, axis=0) * got_ref[k, 0:block, :].astype(F32)
+            later = later + logs[k]
+        for z in range(chips):
+            msg_ref[z, c * block : (c + 1) * block, :] = final.astype(BF16)
     later_ref[...] = jnp.concatenate([mine, jnp.zeros((8 - H, DH), F32)], axis=0)
-    final = jnp.concatenate(final, axis=0).astype(BF16)
     sums[...] = jnp.zeros_like(sums)
-    responses = (got_ref.shape[1] - block - 16) // block
-    for k in range(n):
+    for k in range(m):
         for i in range(responses):
-            at = block + 16 + i * block
-            p = jnp.max(notes[k][3 * H + i : 3 * H + i + 1]).astype(jnp.int32)
-            sums[p] += got_ref[k, at : at + block, :].astype(F32)
-    for p in range(count):
-        msg_ref[p, 0:block, :] = final
-        msg_ref[p, block : 2 * block, :] = sums[p].astype(BF16)
-
-
-def third_kernel(n, count, first_ref, got_ref, msg_ref):
-    part = DH // n
-    block = H * part
+            at = block * (1 + i) + 16
+            sums[noted_prompt(notes[k], i)] += got_ref[k, at : at + block, :].astype(F32)
+    for z in range(chips):
+        for c in range(cores):
+            at = (cores + c) * block
+            msg_ref[z, at : at + block, :] = sums[z * cores + c].astype(BF16)
+
+
+def third_kernel(m, chips, first_ref, got_ref, msg_ref):
+    block = H * DH // m
+    cores = got_ref.shape[1] // (2 * block)
     responses = (first_ref.shape[1] - block - 16) // block
-    total = got_ref[0, block:, :].astype(F32)
-    for p in range(1, count):
-        total = total + got_ref[p, block:, :].astype(F32)
-    total = total.astype(BF16)
-    for k in range(n):
+    totals = []
+    for c in range(cores):
+        at = (cores + c) * block
+        total = got_ref[0, at : at + block, :].astype(F32)
+        for z in range(1, chips):
+            total = total + got_ref[z, at : at + block, :].astype(F32)
+        totals.append(total.astype(BF16))
+    for k in range(m):
         notes = first_ref[k, block : block + 16, :].astype(F32)
         for i in range(responses):
-            p = jnp.max(notes[3 * H + i : 3 * H + i + 1]).astype(jnp.int32)
-            msg_ref[k, i * block : (i + 1) * block, :] = got_ref[p, 0:block, :]
-        msg_ref[k, responses * block :, :] = total
+            p = noted_prompt(notes, i)
+            at = pl.multiple_of(lax.rem(p, cores) * block, block)
+            msg_ref[k, i * block : (i + 1) * block, :] = got_ref[lax.div(p, cores), pl.ds(at, block), :]
+        msg_ref[k, responses * block :, :] = totals[k % cores]
 
 
 def sweep_kernel(cols_ref, rows_ref, q_ref, k_ref, v_ref, c_ref, out_ref, dq_ref, dk_ref, dv_ref):
@@ -210,15 +228,13 @@
 
 
 def last_kernel(
-    n, steps, cols_ref, q_ref, c_ref, po_ref, pdq_ref, got_ref, keys_ref, values_ref, suffix_ref, later_ref,
-    out_ref, dq_ref, dk_ref, dv_ref, start,
+    m, steps, cols_ref, q_ref, c_ref, po_ref, pdq_ref, got_ref, keys_ref, values_ref, suffix_ref, later_ref,
+    out_ref, dq_ref, dk_ref, dv_ref,
 ):
     r = pl.program_id(0)
-    part = DH // n
-    for k in range(n):
-        for h in range(H):
-            at = pl.multiple_of((r * H + h) * part, part)
-            start[h, k * part : (k + 1) * part, :] = got_ref[k, pl.ds(at, part), :]
+    block = H * DH // m
+    blocks = [got_ref[k, pl.ds(pl.multiple_of(r * block, block), block), :] for k in range(m)]
+    start = [from_blocks(blocks, h) for h in range(H)]
     mine = pltpu.roll(cols_ref[...], lax.rem(128 - 8 * r, 128), 1)
     live = mine[:, 4:5]
     opened = mine[:, 5:6]
@@ -233,10 +249,10 @@
 
     @pl.when(r == 0)
     def _():
+        blocks = [got_ref[k, steps * block : (steps + 1) * block, :] for k in range(m)]
         for h in range(H):
             lanes = slice(h * DH, (h + 1) * DH)
-            at = (steps * H + h) * part
-            grad = jnp.concatenate([got_ref[k, at : at + part, :] for k in range(n)], axis=0)
+            grad = from_blocks(blocks, h)
             factor = jnp.exp(suffix_ref[:, h : h + 1] + later_ref[h : h + 1, 0:1])
             dk_ref[0, :, lanes] = (factor * mm_nt(values_ref[0, :, lanes], grad)).astype(BF16)
             dv_ref[0, :, lanes] = (factor * mm(keys_ref[0, :, lanes], grad)).astype(BF16)
@@ -260,19 +276,21 @@
     loss_mask,
     advantages,
 ):
-    n = lax.axis_size("prompt")
-    count = lax.axis_size("resp")
-    row = lax.axis_index("prompt").astype(jnp.int32)[None]
+    plane = ("prompt", "core")
+    cores = lax.axis_size("core")
+    chips = lax.axis_size("z")
+    m = lax.axis_size("prompt") * cores
+    place = lax.axis_index(plane).astype(jnp.int32)[None]
     responses, slots, width = queries.shape
-    block_rows = H * DH // n
+    block_rows = H * DH // m
     tokens = keys.shape[1]
     shape = jax.ShapeDtypeStruct
     HBM = pl.BlockSpec(memory_space=pltpu.HBM)
 
     msg, suffix, cols, rows = pl.pallas_call(
-        lambda *refs: first_kernel(n, *refs),
+        lambda *refs: first_kernel(m, *refs),
         out_shape=[
-            shape((n, block_rows * (1 + responses) + 16, DH), BF16),
+            shape((m, block_rows * (1 + responses) + 16, DH), BF16),
             shape((tokens, 128), F32),
             shape((slots, 128), F32),
             shape((responses, 8, slots), F32),
@@ -294,26 +312,26 @@
     )(
         group_ids, resp_lengths, advantages, keys, values, prompt_gates, resp_gates, loss_mask, queries, cotangent
     )
-    got1 = exchange(msg, "prompt")
+    got1 = exchange(msg, plane)
     msg, later = pl.pallas_call(
-        lambda *refs: second_kernel(n, count, *refs),
-        out_shape=[shape((count, 2 * block_rows, DH), BF16), shape((8, DH), F32)],
+        lambda *refs: second_kernel(m, chips, *refs),
+        out_shape=[shape((chips, 2 * cores * block_rows, DH), BF16), shape((8, DH), F32)],
         in_specs=[SMEM, VMEM],
         out_specs=[VMEM, VMEM],
-        scratch_shapes=[pltpu.VMEM((count, block_rows, DH), F32)],
+        scratch_shapes=[pltpu.VMEM((chips * cores, block_rows, DH), F32)],
         compiler_params=params(16),
         name="second",
-    )(row, got1)
-    got2 = exchange(msg, "resp")
+    )(place, got1)
+    got2 = exchange(msg, "z")
     msg = pl.pallas_call(
-        lambda *refs: third_kernel(n, count, *refs),
-        out_shape=shape((n, (responses + 1) * block_rows, DH), BF16),
+        lambda *refs: third_kernel(m, chips, *refs),
+        out_shape=shape((m, (responses + 1) * block_rows, DH), BF16),
         in_specs=[VMEM, VMEM],
         out_specs=VMEM,
         compiler_params=params(16),
         name="third",
     )(got1, got2)
-    got3 = exchange(msg, "prompt")
+    got3 = exchange(msg, plane)
 
     block = pl.BlockSpec((1, slots, width), lambda r: (r, 0, 0))
     lane_block = pl.BlockSpec((slots, 128), lambda r: (0, 0))
@@ -331,12 +349,11 @@
     )(cols, rows, queries, resp_keys, resp_values, cotangent)
 
     resp_out, resp_dq, prompt_dk, prompt_dv = pl.pallas_call(
-        lambda *refs: last_kernel(n, responses, *refs),
+        lambda *refs: last_kernel(m, responses, *refs),
         grid=(responses,),
         out_shape=[like_out, like_out, shape(keys.shape, BF16), shape(keys.shape, BF16)],
         in_specs=[lane_block, block, block, block, block] + [VMEM] * 5,
         out_specs=[block, block, VMEM, VMEM],
-        scratch_shapes=[pltpu.VMEM((H, DH, DH), BF16)],
         compiler_params=params(),
         name="last",
     )(cols, queries, cotangent, partial_out, partial_dq, got3, keys, values, suffix, later)
@@ -344,17 +361,20 @@
 
 
 def solution(mesh):
-    spread = P(("prompt", "resp"))
-    three = P(("prompt", "resp"), None, None)
-    two = P(("prompt", "resp"), None)
-    prompt = P("resp", "prompt", None)
+    n, count = mesh.shape["prompt"], mesh.shape["resp"]
+    cores = 2 if count % 2 == 0 else 1
+    mesh = jax.sharding.Mesh(mesh.devices.reshape(n, count // cores, cores), ("prompt", "z", "core"))
+    spread = P(("prompt", "z", "core"))
+    three = P(("prompt", "z", "core"), None, None)
+    two = P(("prompt", "z", "core"), None)
+    prompt = P(("z", "core"), "prompt", None)
     return jax.shard_map(
         shards,
         mesh=mesh,
         in_specs=(
             prompt,
             prompt,
-            P("resp", None, "prompt"),
+            P(("z", "core"), None, "prompt"),
             three,
             three,
             three,

time: 56.5 us -> 54.9 us (0.972)
  blocking collectives: 14.4 us -> 10.6 us
  waiting for transfers between devices: 6.05 us -> 7.99 us
    all_to_all x1, blocking collectives: 14.4 us -> 10.6 us  [exchange(): return lax.all_to_all(x, axis, 0, 0, tiled=True)]
    all_to_all x2, waiting for transfers between devices: 6.05 us -> 7.99 us  [exchange(): return lax.all_to_all(x, axis, 0, 0, tiled=True)]
  transfers between devices with their start and end apart: 2 -> 2, of which waited for: 1 -> 1; matrix products, arithmetic and copies ran while one was open for 0% -> 0% of each run, Pallas kernels for 21% -> 22%
where the time goes in v1:
time: 54.9 us; the launch traced here: 54.5 us
  Pallas kernels  25.3 us (46%)
  blocking collectives  10.6 us (19%)
  starting transfers between devices  8.62 us (16%)
  waiting for transfers between devices  7.99 us (15%)
  local copies, waits for them, and re-layouts  1.29 us (2%)
  between operations  0.68 us (1%)
    pallas_call x1, Pallas kernels, shards(): pl.pallas_call(sweep_kernel, grid=(responses,), out_shape=[like, like, li...  11.8 us
    all_to_all x1, blocking collectives, exchange(): return lax.all_to_all(x, axis, 0, 0, tiled=True)  10.6 us
    all_to_all x2, starting transfers between devices, exchange(): return lax.all_to_all(x, axis, 0, 0, tiled=True)  8.62 us
    all_to_all x2, waiting for transfers between devices, exchange(): return lax.all_to_all(x, axis, 0, 0, tiled=True)  7.99 us
    pallas_call x1, Pallas kernels, shards(): pl.pallas_call(lambda *refs: first_kernel(m, *refs), out_shape=[shape((m,...  6.11 us
    pallas_call x1, Pallas kernels, shards(): pl.pallas_call(lambda *refs: last_kernel(m, responses, *refs), grid=(resp...  6.03 us
    unnamed x4, local copies, waits for them, and re-layouts  1.29 us
  transfers between devices with their start and end apart: 2, of which 1 were waited for; matrix products, arithmetic and copies ran while one was open for 0% of the time, Pallas kernels for 22%

profile of v1, /device:TPU:0, one launch (start us, length us, event | category | flops | bytes accessed | tf_op | source)
XLA Modules:
  0.0 54.5 jit_solution(13637920800478676295)
XLA Ops:
  0.6 6.1 %first.1 = (bf16[8,176,128]{2,1,0:T(8,128)(2,1)}, f32[256,128]{1,0:T(8,128)}, f32[512,128]{1,0:T(8,128)}, f32[4,8,512]{2,1,0:T(8,128)}) custom-call(s32[4]{0:T(128)} %refs_0_.1, s32[1,4]{1,0:T(1,128)} %refs_1_.2, s32[4]{0:T(128)} %refs_2_.2, bf16[1,256,256]{2,1,0:T(8,128)(2,1)} %refs_6_.3, bf16[1,256,256]{2,1,0:T(8,128)(2,1)} %refs_7_.3, ...), custom_call_target="tpu_custom_call" | custom-call | tf_op jit(solution)/shard_map/first/pallas_call | solution.py:290
  6.8 5.2 %all-to-all-start = ((bf16[8,176,128]{2,1,0:T(8,128)(2,1)}), bf16[8,176,128]{2,1,0:T(8,128)(2,1)S(1)}, u32[]{:S(2)}, u32[]{:S(2)}) async-start(bf16[8,176,128]{2,1,0:T(8,128)(2,1)} %get-tuple-element.24), calls=%async_computation | async-start | bytes 720896 | tf_op jit(solution)/shard_map/all_to_all | solution.py:262
  11.9 8.0 %all-to-all-done.refs_1_.refs_0_ = bf16[8,176,128]{2,1,0:T(8,128)(2,1)S(1)} async-done(((bf16[8,176,128]{2,1,0:T(8,128)(2,1)}), bf16[8,176,128]{2,1,0:T(8,128)(2,1)S(1)}, u32[]{:S(2)}, u32[]{:S(2)}) %all-to-all-start) | async-done | bytes 360480 | tf_op jit(solution)/shard_map/all_to_all | solution.py:262
  19.9 0.3 second.1
  20.3 0.0 copy-start
  20.3 0.6 %copy-done = f32[8,128]{1,0:T(8,128)} copy-done((f32[8,128]{1,0:T(8,128)}, f32[8,128]{1,0:T(8,128)S(1)}, u32[]{:S(2)}) %copy-start) | copy-done | bytes 4120
  20.9 10.6 %all_to_all.15.refs_1_ = bf16[4,128,128]{2,1,0:T(8,128)(2,1)S(1)} all-to-all(bf16[4,128,128]{2,1,0:T(8,128)(2,1)S(1)} %get-tuple-element.25), channel_id=1, replica_groups=mesh['prompt'=4,'z'=4,'core'=2] {'z'}, dimensions={0} | all-to-all | bytes 262144 | tf_op jit(solution)/shard_map/all_to_all | solution.py:262
  31.4 1.0 %third.1 = bf16[8,160,128]{2,1,0:T(8,128)(2,1)} custom-call(bf16[8,176,128]{2,1,0:T(8,128)(2,1)S(1)} %all-to-all-done.refs_1_.refs_0_, bf16[4,128,128]{2,1,0:T(8,128)(2,1)S(1)} %all_to_all.15.refs_1_), custom_call_target="tpu_custom_call" | custom-call | tf_op jit(solution)/shard_map/third/pallas_call | solution.py:326
  32.5 3.4 %all-to-all-start.2 = ((bf16[8,160,128]{2,1,0:T(8,128)(2,1)}), bf16[8,160,128]{2,1,0:T(8,128)(2,1)S(1)}, u32[]{:S(2)}, u32[]{:S(2)}) async-start(bf16[8,160,128]{2,1,0:T(8,128)(2,1)} %third.1), calls=%async_computation.2 | async-start | bytes 655360 | tf_op jit(solution)/shard_map/all_to_all | solution.py:262
  35.9 11.8 %sweep.1 = (f32[4,512,256]{2,1,0:T(8,128)}, f32[4,512,256]{2,1,0:T(8,128)}, bf16[4,512,256]{2,1,0:T(8,128)(2,1)}, bf16[4,512,256]{2,1,0:T(8,128)(2,1)}) custom-call(f32[512,128]{1,0:T(8,128)} %get-tuple-element.20.cols_ref.refs_0_, f32[4,8,512]{2,1,0:T(8,128)} %get-tuple-element.21.rows_ref, bf16[4,512,256]{2,1,0:T(8,128)(2,1)} %refs_1_.3, ...), custom_call_target="tpu_custom_call" | custom-call | tf_op jit(solution)/shard_map/sweep/pallas_call | solution.py:341
  47.7 0.0 all-to-all-done.2.refs_5_
  47.7 0.0 copy-start.1
  47.7 0.7 %copy-done.1 = bf16[8,160,128]{2,1,0:T(8,128)(2,1)} copy-done((bf16[8,160,128]{2,1,0:T(8,128)(2,1)}, bf16[8,160,128]{2,1,0:T(8,128)(2,1)S(1)}, u32[]{:S(2)}) %copy-start.1) | copy-done | bytes 327704
  48.4 6.0 %last.1 = (bf16[4,512,256]{2,1,0:T(8,128)(2,1)}, bf16[4,512,256]{2,1,0:T(8,128)(2,1)}, bf16[1,256,256]{2,1,0:T(8,128)(2,1)}, bf16[1,256,256]{2,1,0:T(8,128)(2,1)}) custom-call(f32[512,128]{1,0:T(8,128)} %get-tuple-element.20.cols_ref.refs_0_, bf16[4,512,256]{2,1,0:T(8,128)(2,1)} %refs_1_.3, bf16[4,512,256]{2,1,0:T(8,128)(2,1)} %refs_2_.3, ...), custom_call_target="tpu_custom_call" | custom-call | tf_op jit(solution)/shard_map/last/pallas_call | solution.py:351
Async XLA Ops:
  6.8 13.2 %all-to-all-start = ((bf16[8,176,128]{2,1,0:T(8,128)(2,1)}), bf16[8,176,128]{2,1,0:T(8,128)(2,1)S(1)}, u32[]{:S(2)}, u32[]{:S(2)}) async-start(bf16[8,176,128]{2,1,0:T(8,128)(2,1)} %get-tuple-element.24), calls=%async_computation | async-start | bytes 720896 | tf_op jit(solution)/shard_map/all_to_all | solution.py:262
  20.3 0.6 %copy-start = (f32[8,128]{1,0:T(8,128)}, f32[8,128]{1,0:T(8,128)S(1)}, u32[]{:S(2)}) copy-start(f32[8,128]{1,0:T(8,128)S(1)} %get-tuple-element.27.refs_9_) | copy-start | bytes 12292
  32.5 15.3 %all-to-all-start.2 = ((bf16[8,160,128]{2,1,0:T(8,128)(2,1)}), bf16[8,160,128]{2,1,0:T(8,128)(2,1)S(1)}, u32[]{:S(2)}, u32[]{:S(2)}) async-start(bf16[8,160,128]{2,1,0:T(8,128)(2,1)} %third.1), calls=%async_computation.2 | async-start | bytes 655360 | tf_op jit(solution)/shard_map/all_to_all | solution.py:262
  47.7 0.7 %copy-start.1 = (bf16[8,160,128]{2,1,0:T(8,128)(2,1)}, bf16[8,160,128]{2,1,0:T(8,128)(2,1)S(1)}, u32[]{:S(2)}) copy-start(bf16[8,160,128]{2,1,0:T(8,128)(2,1)S(1)} %all-to-all-done.2.refs_5_) | copy-start | bytes 983044
